TPU v7x, 128 devices: a whole 4x4x4 slice. The times are simulated.
128 devices in a mesh: row: 8 (over y, core), col: 16 (over z, x).
Axes of the slice: x: 4, y: 4, z: 4, core: 2. Of those that a mesh axis runs over, the one named last changes fastest.
Arguments:
- factor: float32 [256, 1536, 1536], P(('row', 'col'))
- coupling: bfloat16 [256, 1536, 512], P(('row', 'col')), may hold values from -0.15625 to 0.15625
- boundary: float32 [256, 512, 512], P(('row', 'col'))
- loads: float32 [32, 16384], P(None, ('row', 'col')), may hold values from -6 to 6
- block_ids: int32 [256, 16], P(('row', 'col')), may hold values from 0 to 511, as said below
- live_counts: int32 [256], P(('row', 'col')), may hold values from 8 to 16
Outputs:
- response: float32 [32, 16384], P(None, ('row', 'col'))
Inputs may be any that keep to these rules, and one draw needn't show every extreme that they name: `block_ids`: district d lies on device d // 2 (rows then columns of the mesh); its slot s names a block owned by the device in the same mesh row and in mesh column s % 16, where device p owns blocks p * 4 to p * 4 + 3.
All inputs are finite; a program needn't handle non-finite values.
Results may differ from a plain program's by a relative error of at most 0.0003.
Values sent between devices are 32-bit elements; how exact they have to be, the bound alone decides.
No kernel may reach another device: no remote copies, remote signals or barrier semaphores. Data moves between devices by JAX's collectives and lax.ppermute only.
A program may use at most 128 MiB of HBM per device.

v0:
```python
import jax
import jax.numpy as jnp
from jax import lax
from jax.sharding import PartitionSpec as P

BS = 32


def district_image(factor, coupling, boundary, picked, live_count):
    solved = jax.scipy.linalg.solve_triangular(factor, coupling.astype(jnp.float32), lower=True)
    schur_block = boundary - lax.dot_general(
        solved,
        solved,
        (((0,), (0,)), ((), ())),
        precision=lax.Precision.HIGHEST,
        preferred_element_type=jnp.float32,
    )
    weights = (jnp.arange(picked.shape[1]) < live_count).astype(jnp.float32)
    masked = (picked * weights[None, :, None]).reshape(picked.shape[0], -1)
    image = lax.dot_general(
        masked,
        schur_block,
        (((1,), (1,)), ((), ())),
        precision=lax.Precision.HIGHEST,
        preferred_element_type=jnp.float32,
    )
    return image.reshape(picked.shape) * weights[None, :, None]


def body(factor, coupling, boundary, loads, block_ids, live_counts):
    cases = loads.shape[0]
    gathered = lax.all_gather(loads, "col", axis=1, tiled=True)
    offset = lax.axis_index("row") * (gathered.shape[1] // BS)
    load_table = gathered.reshape(cases, -1, BS)
    images = []
    for district in range(factor.shape[0]):
        picked = jnp.take(load_table, block_ids[district] - offset, axis=1)
        images.append(
            district_image(
                factor[district],
                coupling[district],
                boundary[district],
                picked,
                live_counts[district],
            )
        )
    images = jnp.concatenate(images, axis=1)
    flat_ids = block_ids.reshape(-1)
    block_total = load_table.shape[1]
    onehot = ((flat_ids - offset)[:, None] == jnp.arange(block_total)[None, :]).astype(jnp.float32)
    dense_term = jnp.einsum("rsb,sj->rjb", images, onehot, precision=lax.Precision.HIGHEST).reshape(
        cases, -1
    )
    return lax.psum_scatter(dense_term, "col", scatter_dimension=1, tiled=True)


def solution(mesh):
    placed = (
        P(("row", "col"), None, None),
        P(("row", "col"), None, None),
        P(("row", "col"), None, None),
        P(None, ("row", "col")),
        P(("row", "col"), None),
        P(("row", "col")),
    )
    return jax.shard_map(
        body, mesh=mesh, in_specs=placed, out_specs=P(None, ("row", "col")), check_vma=False
    )
```

profile of v0, /device:TPU:0, one launch (start us, length us, event | category | flops | bytes accessed | tf_op | source)
XLA Modules:
  0.0 552.0 jit_solution(11103956469716437403)
XLA Ops:
  8.0 14.9 %bitcast_select_fusion.1 = (f32[1536,1536]{1,0:T(8,128)}, f32[1536,1536]{1,0:T(8,128)}) fusion(f32[2,1536,1536]{2,1,0:T(8,128)} %param.10), kind=kLoop, calls=%fused_computation.7 | loop fusion | flops 7077888 | bytes 37748736 | tf_op jit(solution)/shard_map/jit(_solve_triangular)/triangular_solve | solution.py:10
  23.9 40.8 %while.4 = (s32[]{:T(128)}, f32[1536,1536]{1,0:T(8,128)}, s32[12,2]{0,1:T(2,128)S(1)}, f32[12,128,128]{2,1,0:T(8,128)}, s32[]{:T(128)}) while((s32[]{:T(128)}, f32[1536,1536]{1,0:T(8,128)}, s32[12,2]{0,1:T(2,128)S(1)}, f32[12,128,128]{2,1,0:T(8,128)}, s32[]{:T(128)}) %tuple.167), condition=%wide.while_cond, body=%wide.while_body.sunk | while | flops 2 | bytes 132705 | solution.py:10
  24.5 2.8 bitcast_dynamic-update-slice_fusion.4
  27.9 2.8 bitcast_dynamic-update-slice_fusion.4
  31.3 2.8 bitcast_dynamic-update-slice_fusion.4
  34.7 2.8 bitcast_dynamic-update-slice_fusion.4
  38.1 2.8 bitcast_dynamic-update-slice_fusion.4
  41.5 2.8 bitcast_dynamic-update-slice_fusion.4
  44.9 2.8 bitcast_dynamic-update-slice_fusion.4
  48.3 2.8 bitcast_dynamic-update-slice_fusion.4
  51.8 2.8 bitcast_dynamic-update-slice_fusion.4
  55.2 2.8 bitcast_dynamic-update-slice_fusion.4
  58.6 2.8 bitcast_dynamic-update-slice_fusion.4
  62.0 2.8 bitcast_dynamic-update-slice_fusion.4
  64.7 119.5 %custom-call.4 = f32[12,128,128]{1,2,0:T(8,128)} custom-call(f32[12,128,128]{2,1,0:T(8,128)} %get-tuple-element.21), custom_call_target="InvertDiagBlocksLowerTriangular" | custom-call | tf_op jit(solution)/shard_map/jit(_solve_triangular)/triangular_solve | solution.py:10
  184.2 2.6 bitcast_convert_fusion.1
  200.3 2.2 convolution_subtract_fusion.10
  203.0 2.3 convolution_subtract_fusion.9
  205.9 2.6 convolution_subtract_fusion.17
  208.9 3.1 convolution_subtract_fusion.22
  212.4 3.6 convolution_subtract_fusion.8
  216.0 25.4 %all_gather.3 = f32[32,2048]{1,0:T(8,128)S(1)} all-gather(f32[32,128]{1,0:T(8,128)S(1)} %copy-done.7), channel_id=1, replica_groups=mesh['row'=8,'col'=16] {'col'}, dimensions={1}, use_global_device_ids=true | all-gather | bytes 278528 | tf_op jit(solution)/shard_map/all_gather | solution.py:32
  242.7 2.8 copy.7
  253.1 2.3 bitcast_multiply_fusion
  258.2 6.4 %convolution_subtract_fusion.1 = f32[512,512]{1,0:T(8,128)S(1)} fusion(f32[1536,512]{1,0:T(8,128)S(1)} %convolution_dynamic-update-slice_fusion.1, f32[2,512,512]{2,1,0:T(8,128)} %param.12), kind=kOutput, calls=%fused_computation.12 | convolution fusion | flops 4832100352 | bytes 8388608 | tf_op jit(solution)/shard_map/dot_general | solution.py:11
  264.6 2.5 fusion.87
  271.0 42.2 %while.5 = (s32[]{:T(128)}, f32[1536,1536]{1,0:T(8,128)}, s32[12,2]{0,1:T(2,128)S(1)}, f32[12,128,128]{2,1,0:T(8,128)}, s32[]{:T(128)}) while((s32[]{:T(128)}, f32[1536,1536]{1,0:T(8,128)}, s32[12,2]{0,1:T(2,128)S(1)}, f32[12,128,128]{2,1,0:T(8,128)}, s32[]{:T(128)}) %tuple.172), condition=%wide.while_cond.clone, body=%wide.while_body.clone.sunk | while | flops 2 | bytes 132705 | solution.py:10
  271.6 2.9 bitcast_dynamic-update-slice_fusion.5
  275.1 2.9 bitcast_dynamic-update-slice_fusion.5
  278.7 2.9 bitcast_dynamic-update-slice_fusion.5
  282.2 2.9 bitcast_dynamic-update-slice_fusion.5
  285.7 2.9 bitcast_dynamic-update-slice_fusion.5
  289.2 2.9 bitcast_dynamic-update-slice_fusion.5
  292.7 2.9 bitcast_dynamic-update-slice_fusion.5
  296.3 2.9 bitcast_dynamic-update-slice_fusion.5
  299.8 2.9 bitcast_dynamic-update-slice_fusion.5
  303.3 2.9 bitcast_dynamic-update-slice_fusion.5
  306.8 2.9 bitcast_dynamic-update-slice_fusion.5
  310.3 2.9 bitcast_dynamic-update-slice_fusion.5
  313.2 119.5 %custom-call.5 = f32[12,128,128]{1,2,0:T(8,128)} custom-call(f32[12,128,128]{2,1,0:T(8,128)} %get-tuple-element.22), custom_call_target="InvertDiagBlocksLowerTriangular" | custom-call | tf_op jit(solution)/shard_map/jit(_solve_triangular)/triangular_solve | solution.py:10
  447.0 2.2 convolution_subtract_fusion.4
  449.8 2.3 convolution_subtract_fusion.3
  452.6 2.6 convolution_subtract_fusion.14
  455.6 2.9 convolution_subtract_fusion.20
  459.0 3.1 convolution_subtract_fusion.2
  462.5 5.4 convolution_subtract_fusion
  468.3 2.5 fusion.88
  473.3 71.6 %reduce-scatter.2.cloned.1.call-done = f32[32,128]{1,0:T(8,128)} async-done(((f32[32,2048]{1,0:T(8,128)}), f32[32,128]{1,0:T(8,128)}) %reduce-scatter.2.cloned.1.call-update) | async-done | bytes 16400 | tf_op jit(solution)/shard_map/reduce_scatter | solution.py:54
  (133 shorter events, 67.1 us)
Async XLA Ops:
  6.5 538.4 %reduce-scatter.2.cloned.1.call-start = ((), (), s32[]{:S(2)}) async-start(), calls=%async_computation.1 | async-start | bytes 278528 | tf_op jit(solution)/shard_map/reduce_scatter | solution.py:54
  8.0 176.2 %copy-start.1 = (bf16[2,1536,512]{2,1,0:T(8,128)(2,1)S(1)}, bf16[2,1536,512]{2,1,0:T(8,128)(2,1)}, u32[]{:S(2)}) copy-start(bf16[2,1536,512]{2,1,0:T(8,128)(2,1)} %param.11) | copy-start | bytes 9437188
  184.2 2.6 copy-start.5
  212.0 4.1 copy-start.7
  242.7 8.5 %copy-start.8 = (s32[2]{0:T(128)S(1)}, s32[2]{0:T(128)}, u32[]{:S(2)}) copy-start(s32[2]{0:T(128)} %param.15) | copy-start | bytes 28
  264.6 168.1 %copy-start = (f32[1536,512]{1,0:T(8,128)S(1)}, f32[1536,512]{1,0:T(8,128)}, u32[]{:S(2)}) copy-start(f32[1536,512]{1,0:T(8,128)} %get-tuple-element.50) | copy-start | bytes 9437188
  432.7 2.7 copy-start.6
  458.5 4.0 copy-start.4
  462.5 5.4 copy-start.2
  467.9 3.2 copy-start.3
Sparse Core Ops, SparseCore 0:
  473.5 71.3 reduce-scatter.1
where the time goes:
time: 557 us; the launch traced here: 552 us
  other arithmetic  264 us (47%)
  local copies, waits for them, and re-layouts  100 us (18%)
  matrix products  77.2 us (14%)
  waiting for transfers between devices  71.6 us (13%)
  blocking collectives  25.4 us (5%)
  between operations  14.2 us (3%)
    another operation x4, other arithmetic, district_image(): jax.scipy.linalg.solve_triangular(factor, coupling.astype(jnp.float32), l...  254 us
    another operation x75, local copies, waits for them, and re-layouts, district_image(): jax.scipy.linalg.solve_triangular(factor, coupling.astype(jnp.float32), l...  84.9 us
    reduce_scatter x1, waiting for transfers between devices, body(): return lax.psum_scatter(dense_term, 'col', scatter_dimension=1, tiled=True)  71.6 us
    another operation x46, matrix products, district_image(): jax.scipy.linalg.solve_triangular(factor, coupling.astype(jnp.float32), l...  60 us
    all_gather x1, blocking collectives, body(): gathered = lax.all_gather(loads, 'col', axis=1, tiled=True)  25.4 us
    dot_general x2, matrix products, district_image(): lax.dot_general(solved, solved, (((0,), (0,)), ((), ())), precision=lax.P...  11.8 us
  transfers between devices with their start and end apart: 1, of which 1 were waited for; matrix products, arithmetic and copies ran while one was open for 0% of the time, Pallas kernels for 0%

commit v1 on v0

--- a/solution.py
+++ b/solution.py
@@ -29,7 +29,10 @@
 
 def body(factor, coupling, boundary, loads, block_ids, live_counts):
     cases = loads.shape[0]
-    gathered = lax.all_gather(loads, "col", axis=1, tiled=True)
+    size = lax.axis_size("col")
+    blocks = jnp.stack([loads for _ in range(size)])
+    blocks = lax.all_to_all(blocks, "col", split_axis=0, concat_axis=0)
+    gathered = jnp.concatenate(blocks, axis=1)
     offset = lax.axis_index("row") * (gathered.shape[1] // BS)
     load_table = gathered.reshape(cases, -1, BS)
     images = []

time: 557 us -> 535 us (0.961)
  blocking collectives: 25.4 us -> 0 us
  starting transfers between devices: 0.01 us -> 8.05 us
    all_gather x1 -> x0, blocking collectives: 25.4 us -> none  [body(): gathered = lax.all_gather(loads, 'col', axis=1, tiled=True)]
    all_to_all x0 -> x1, starting transfers between devices: none -> 8.01 us  [body(): blocks = lax.all_to_all(blocks, 'col', split_axis=0, concat_axis=0)]
  transfers between devices with their start and end apart: 1 -> 2, of which waited for: 1 -> 1; matrix products, arithmetic and copies ran while one was open for 0% -> 79% of each run, Pallas kernels for 0% -> 0%
where the time goes in v1:
time: 535 us; the launch traced here: 529 us
  other arithmetic  259 us (48%)
  local copies, waits for them, and re-layouts  97.2 us (18%)
  matrix products  76.6 us (14%)
  waiting for transfers between devices  74 us (14%)
  between operations  14.2 us (3%)
  starting transfers between devices  8.05 us (2%)
    another operation x4, other arithmetic, district_image(): jax.scipy.linalg.solve_triangular(factor, coupling.astype(jnp.float32), l...  254 us
    another operation x75, local copies, waits for them, and re-layouts, district_image(): jax.scipy.linalg.solve_triangular(factor, coupling.astype(jnp.float32), l...  86 us
    reduce_scatter x1, waiting for transfers between devices, body(): return lax.psum_scatter(dense_term, 'col', scatter_dimension=1, tiled=True)  74 us
    another operation x46, matrix products, district_image(): jax.scipy.linalg.solve_triangular(factor, coupling.astype(jnp.float32), l...  59.5 us
    dot_general x2, matrix products, district_image(): lax.dot_general(solved, solved, (((0,), (0,)), ((), ())), precision=lax.P...  11.8 us
  transfers between devices with their start and end apart: 2, of which 1 were waited for; matrix products, arithmetic and copies ran while one was open for 79% of the time, Pallas kernels for 0%

profile of v1, /device:TPU:0, one launch (start us, length us, event | category | flops | bytes accessed | tf_op | source)
XLA Modules:
  0.0 529.4 jit_solution(12180967756184603346)
XLA Ops:
  8.0 8.0 %all-to-all-start = ((f32[16,32,128]{2,1,0:T(8,128)}), f32[16,32,128]{2,1,0:T(8,128)}, u32[]{:S(2)}, u32[]{:S(2)}) async-start(f32[16,32,128]{2,1,0:T(8,128)} %stack.2), calls=%async_computation | async-start | bytes 524288 | tf_op jit(solution)/shard_map/all_to_all | solution.py:34
  17.5 14.9 %bitcast_select_fusion.1 = (f32[1536,1536]{1,0:T(8,128)}, f32[1536,1536]{1,0:T(8,128)}) fusion(f32[2,1536,1536]{2,1,0:T(8,128)} %param.10), kind=kLoop, calls=%fused_computation.7 | loop fusion | flops 7077888 | bytes 37748736 | tf_op jit(solution)/shard_map/jit(_solve_triangular)/triangular_solve | solution.py:10
  33.4 40.8 %while.4 = (s32[]{:T(128)}, f32[1536,1536]{1,0:T(8,128)}, s32[12,2]{0,1:T(2,128)S(1)}, f32[12,128,128]{2,1,0:T(8,128)}, s32[]{:T(128)}) while((s32[]{:T(128)}, f32[1536,1536]{1,0:T(8,128)}, s32[12,2]{0,1:T(2,128)S(1)}, f32[12,128,128]{2,1,0:T(8,128)}, s32[]{:T(128)}) %tuple.167), condition=%wide.while_cond, body=%wide.while_body.sunk | while | flops 2 | bytes 132705 | solution.py:10
  34.0 2.8 bitcast_dynamic-update-slice_fusion.4
  37.4 2.8 bitcast_dynamic-update-slice_fusion.4
  40.8 2.8 bitcast_dynamic-update-slice_fusion.4
  44.2 2.8 bitcast_dynamic-update-slice_fusion.4
  47.6 2.8 bitcast_dynamic-update-slice_fusion.4
  51.0 2.8 bitcast_dynamic-update-slice_fusion.4
  54.5 2.8 bitcast_dynamic-update-slice_fusion.4
  57.9 2.8 bitcast_dynamic-update-slice_fusion.4
  61.3 2.8 bitcast_dynamic-update-slice_fusion.4
  64.7 2.8 bitcast_dynamic-update-slice_fusion.4
  68.1 2.8 bitcast_dynamic-update-slice_fusion.4
  71.5 2.8 bitcast_dynamic-update-slice_fusion.4
  74.2 119.5 %custom-call.4 = f32[12,128,128]{1,2,0:T(8,128)} custom-call(f32[12,128,128]{2,1,0:T(8,128)} %get-tuple-element.21), custom_call_target="InvertDiagBlocksLowerTriangular" | custom-call | tf_op jit(solution)/shard_map/jit(_solve_triangular)/triangular_solve | solution.py:10
  193.8 2.6 bitcast_convert_fusion.1
  207.3 2.0 convolution_subtract_fusion.18
  209.8 2.2 convolution_subtract_fusion.10
  212.6 2.3 convolution_subtract_fusion.9
  215.4 2.6 convolution_subtract_fusion.17
  218.4 3.1 convolution_subtract_fusion.22
  221.9 2.9 convolution_subtract_fusion.8
  227.0 43.3 %while.5 = (s32[]{:T(128)}, f32[1536,1536]{1,0:T(8,128)}, s32[12,2]{0,1:T(2,128)S(1)}, f32[12,128,128]{2,1,0:T(8,128)}, s32[]{:T(128)}) while((s32[]{:T(128)}, f32[1536,1536]{1,0:T(8,128)}, s32[12,2]{0,1:T(2,128)S(1)}, f32[12,128,128]{2,1,0:T(8,128)}, s32[]{:T(128)}) %tuple.172), condition=%wide.while_cond.clone, body=%wide.while_body.clone.sunk | while | flops 2 | bytes 132705 | solution.py:10
  227.7 2.9 bitcast_dynamic-update-slice_fusion.5
  231.3 2.9 bitcast_dynamic-update-slice_fusion.5
  234.9 2.9 bitcast_dynamic-update-slice_fusion.5
  238.5 3.0 bitcast_dynamic-update-slice_fusion.5
  242.2 2.9 bitcast_dynamic-update-slice_fusion.5
  245.8 2.9 bitcast_dynamic-update-slice_fusion.5
  249.4 3.0 bitcast_dynamic-update-slice_fusion.5
  253.0 2.9 bitcast_dynamic-update-slice_fusion.5
  256.6 2.9 bitcast_dynamic-update-slice_fusion.5
  260.2 2.9 bitcast_dynamic-update-slice_fusion.5
  263.8 2.9 bitcast_dynamic-update-slice_fusion.5
  267.4 2.9 bitcast_dynamic-update-slice_fusion.5
  270.3 119.3 %custom-call.5 = f32[12,128,128]{1,2,0:T(8,128)} custom-call(f32[12,128,128]{2,1,0:T(8,128)} %get-tuple-element.22), custom_call_target="InvertDiagBlocksLowerTriangular" | custom-call | tf_op jit(solution)/shard_map/jit(_solve_triangular)/triangular_solve | solution.py:10
  401.9 2.0 convolution_subtract_fusion.15
  404.4 2.2 convolution_subtract_fusion.4
  407.2 2.3 convolution_subtract_fusion.3
  410.0 2.6 convolution_subtract_fusion.14
  413.0 2.8 convolution_subtract_fusion.20
  416.3 3.1 convolution_subtract_fusion.2
  420.7 6.2 %convolution_subtract_fusion.1 = f32[512,512]{1,0:T(8,128)} fusion(f32[1536,512]{1,0:T(8,128)S(1)} %convolution_dynamic-update-slice_fusion.1, f32[2,512,512]{2,1,0:T(8,128)S(1)} %copy-done.3), kind=kOutput, calls=%fused_computation.12 | convolution fusion | flops 4832100352 | bytes 8388608 | tf_op jit(solution)/shard_map/dot_general | solution.py:11
  427.3 5.6 %convolution_subtract_fusion = f32[512,512]{1,0:T(8,128)S(1)} fusion(f32[1536,512]{1,0:T(8,128)S(1)} %convolution_dynamic-update-slice_fusion, f32[2,512,512]{2,1,0:T(8,128)S(1)} %copy-done.3), kind=kOutput, calls=%fused_computation.11 | convolution fusion | flops 4832100352 | bytes 8388608 | tf_op jit(solution)/shard_map/dot_general | solution.py:11
  440.9 2.5 convolution_multiply_fusion.1
  443.4 2.5 convolution_multiply_fusion
  448.3 74.0 %reduce-scatter.2.cloned.1.call-done = f32[32,128]{1,0:T(8,128)} async-done(((f32[32,2048]{1,0:T(8,128)}), f32[32,128]{1,0:T(8,128)}) %reduce-scatter.2.cloned.1.call-update) | async-done | bytes 16400 | tf_op jit(solution)/shard_map/reduce_scatter | solution.py:57
  (127 shorter events, 61.0 us)
Async XLA Ops:
  8.0 425.6 %all-to-all-start = ((f32[16,32,128]{2,1,0:T(8,128)}), f32[16,32,128]{2,1,0:T(8,128)}, u32[]{:S(2)}, u32[]{:S(2)}) async-start(f32[16,32,128]{2,1,0:T(8,128)} %stack.2), calls=%async_computation | async-start | bytes 524288 | tf_op jit(solution)/shard_map/all_to_all | solution.py:34
  16.0 506.3 %reduce-scatter.2.cloned.1.call-start = ((), (), s32[]{:S(2)}) async-start(), calls=%async_computation.2 | async-start | bytes 278528 | tf_op jit(solution)/shard_map/reduce_scatter | solution.py:57
  17.5 176.2 %copy-start.2 = (bf16[2,1536,512]{2,1,0:T(8,128)(2,1)S(1)}, bf16[2,1536,512]{2,1,0:T(8,128)(2,1)}, u32[]{:S(2)}) copy-start(bf16[2,1536,512]{2,1,0:T(8,128)(2,1)} %param.11) | copy-start | bytes 9437188
  193.8 2.6 copy-start.4
  221.5 3.4 copy-start.6
  389.7 3.0 copy-start.5
  389.7 3.6 copy-start
  415.8 4.8 copy-start.3
  435.0 5.9 %copy-start.1 = (f32[512,512]{1,0:T(8,128)S(1)}, f32[512,512]{1,0:T(8,128)}, u32[]{:S(2)}) copy-start(f32[512,512]{1,0:T(8,128)} %convolution_subtract_fusion.1) | copy-start | bytes 3145732
Sparse Core Ops, SparseCore 0:
  448.4 73.8 reduce-scatter.1
